TPU v7x, 128 devices: a whole 4x4x4 slice. The times are simulated.
128 devices in a mesh: lon: 32 (over z_lo, y, x), lat: 4 (over z_hi, core).
Axes of the slice: x: 4, y: 4, z: 4 (z_hi: 2, z_lo: 2; z = z_hi * 2 + z_lo), core: 2. Of those that a mesh axis runs over, the one named last changes fastest.
Arguments:
- kernels: float32 [72, 1048576], P(None, ('lon', 'lat')), may hold values from 0.2 to 2
- weighted_residuals: float32 [1048576], P(('lon', 'lat')), may hold values from -6 to 6
- sounding_columns: int32 [1048576], P(('lon', 'lat')), may hold values from 0 to 6143
- segment_counts: int32 [128, 128], P(('lon', 'lat')), may hold values from 0 to 64, as said below
- courant: float32 [2, 72, 1536, 512], P(None, None, 'lon', 'lat'), may hold values from -0.48 to 0.48
- mix_strength: float32 [1536, 512], P('lon', 'lat'), may hold values from 0.05 to 0.6
- cloud_top: int32 [1536, 512], P('lon', 'lat'), may hold values from 1 to 72
- redistribution: float32 [72, 72], replicated, may hold values from -0.75 to 0.75
Outputs:
- sensitivity: float32 [72, 1536, 512], P(None, 'lon', 'lat')
- flux_sensitivity: float32 [1536, 512], P('lon', 'lat')
Inputs may be any that keep to these rules, and one draw needn't show every extreme that they name: `segment_counts`: entry [o, d] is the number of live slots, the first ones, among the 64 slots that retrieval batch o holds for tile d; in every draw one tile gets 64 from every batch, and some batch holds none for some other tile.
All inputs are finite; a program needn't handle non-finite values.
Results may differ from a plain program's by a relative error of at most 0.00013.
Values sent between devices are 32-bit elements; how exact they have to be, the bound alone decides.
A program may use at most 128 MiB of HBM per device.

v0:
```python
import itertools

import jax
import jax.numpy as jnp
from jax import lax
from jax.experimental import pallas as pl
from jax.experimental.pallas import tpu as pltpu
from jax.sharding import PartitionSpec as P

STEPS = 4
LEV = 72
CLON = 48
LANES = 128
CHIPS = 64
DEVICES = 128
ROWS = 37
DEPTH = 224

OFFSETS = sorted(
    itertools.product(range(4), repeat=3), key=lambda o: -sum(min(v, 4 - v) for v in o)
)


def coords():
    lon = lax.axis_index("lon")
    lat = lax.axis_index("lat")
    return lon % 4, (lon // 4) % 4, (lat // 2) * 2 + lon // 16, lat % 2


def at_offset(x, y, z, c):
    mx, my, mz, mc = coords()
    x, y, z, c = (mx + x) % 4, (my + y) % 4, (mz + z) % 4, (mc + c) % 2
    return (z % 2) * 16 + y * 4 + x, (z // 2) * 2 + c


def to(lon, lat):
    return {"lon": lon, "lat": lat}


def iota(shape, dim):
    return lax.broadcasted_iota(jnp.int32, shape, dim)


def split(value):
    high = value.astype(jnp.bfloat16).astype(jnp.float32)
    return high, value - high


def kernel(
    kernels,
    residuals,
    columns,
    counts,
    courant,
    strength,
    cloud_top,
    redistribution,
    out,
    flux,
    forcing_in,
    wind,
    send,
    recv,
    state,
    edge,
    from_south,
    from_north,
    halo,
    mixer,
    load_sem,
    wind_sem,
    send_sem,
    recv_sem,
    edge_send,
    edge_recv,
    out_sem,
):
    lon, lat = lax.axis_index("lon"), lax.axis_index("lat")
    core = lat % 2
    load = pltpu.make_async_copy(kernels, forcing_in, load_sem)
    load.start()
    barrier = pltpu.get_barrier_semaphore()

    def greet(k, carry):
        there = at_offset(k % 4, (k // 4) % 4, (k // 16) % 4, k // 64)
        pl.semaphore_signal(barrier, 1, device_id=to(*there))
        return carry

    lax.fori_loop(1, DEVICES, greet, 0)

    def fetch(i, carry):
        for part in range(2):
            pltpu.make_async_copy(
                courant.at[part, :, i, :], wind.at[part, i], wind_sem
            ).start()
        return carry

    lax.fori_loop(0, CLON, fetch, 0)

    lane = iota((8, LANES), 1)
    sub = iota((8, LANES), 0)
    low = lane < 64

    def lo_half(shape):
        return iota(shape, 1) < 64

    load.wait()
    for m, offset in enumerate(OFFSETS):
        there_lon, there_lat = at_offset(*offset, 0)
        chip = there_lon * 2 + there_lat // 2
        one = counts[0, 2 * chip]
        two = counts[0, 2 * chip + 1]
        row = iota((1, LANES), 1)
        live = (row % 64) < jnp.where(row < 64, one, two)
        weight = jnp.where(live, residuals[pl.ds(chip, 1), :], 0.0)
        place = columns[pl.ds(chip, 1), :].astype(jnp.float32)
        start = pl.multiple_of(chip * LANES, LANES)
        value = forcing_in[:, pl.ds(start, LANES)] * weight
        a, b, last = value[0:32], value[32:64], value[64:72]
        half = lo_half((32, LANES))
        turned = pltpu.roll(last, 4, 0)
        tail_0 = jnp.where(low, last, pltpu.roll(turned, 64, 1))
        tail_1 = jnp.where(low, pltpu.roll(last, 64, 1), turned)
        place_8 = jnp.broadcast_to(place, (8, LANES))
        tail_0 = jnp.where(sub == 4, place_8, tail_0)
        tail_1 = jnp.where(sub == 4, pltpu.roll(place_8, 64, 1), tail_1)
        slot_0 = 2 * m + core
        slot_1 = 2 * m + 1 - core
        send[slot_0, 0:32, :] = jnp.where(half, a, pltpu.roll(b, 64, 1))
        send[slot_1, 0:32, :] = jnp.where(half, pltpu.roll(a, 64, 1), b)
        send[slot_0, 32:ROWS, :] = tail_0[0:5]
        send[slot_1, 32:ROWS, :] = tail_1[0:5]
    mine = DEVICES - 2
    recv[mine] = send[mine]

    def block_copy(k, there):
        return pltpu.make_async_remote_copy(
            src_ref=send.at[k],
            dst_ref=recv.at[k],
            send_sem=send_sem.at[k],
            recv_sem=recv_sem.at[k],
            device_id=to(*there),
        )

    pl.semaphore_wait(barrier, DEVICES - 1)
    for m, offset in enumerate(OFFSETS):
        for c in range(2):
            if 2 * m + c != mine:
                block_copy(2 * m + c, at_offset(*offset, c)).start()

    high, rest = split(redistribution[...].T)
    mixer[...] = jnp.concatenate(
        [high, high, rest, jnp.zeros((LEV, DEPTH - 3 * LEV), jnp.float32)], axis=1
    ).astype(jnp.bfloat16)

    def clear(i, carry):
        state[0, i] = jnp.zeros((LEV, LANES), jnp.float32)
        return carry

    lax.fori_loop(1, CLON + 1, clear, 0)

    def paired(k):
        half = lo_half((32, LANES))
        one, two = recv[k, 0:32, :], recv[k + 1, 0:32, :]
        end_1, end_2 = recv[k, 29:ROWS, :], recv[k + 1, 29:ROWS, :]
        top = jnp.where(half, one, pltpu.roll(two, 64, 1))
        bottom = jnp.where(half, pltpu.roll(one, 64, 1), two)
        end_top = jnp.where(low, end_1, pltpu.roll(end_2, 64, 1))
        end_bottom = jnp.where(low, pltpu.roll(end_1, 64, 1), end_2)
        end = jnp.where(sub < 4, pltpu.roll(end_top, 5, 0), pltpu.roll(end_bottom, 1, 0))
        return jnp.concatenate([top, bottom, end], axis=0), end_top[7:8]

    def gather(t, whole):
        first = 4 * t
        for i in range(4):
            if whole or i != mine % 4:
                block_copy(first + i, (lon, lat)).wait_recv()
        one, place_1 = paired(first)
        two, place_2 = paired(first + 2)
        value = jnp.concatenate([one, two], axis=1)
        place = jnp.concatenate([place_1, place_2], axis=1).astype(jnp.int32)
        high, rest = split(value)
        both = jnp.concatenate([high, rest], axis=0).astype(jnp.bfloat16)
        across = place // 256
        within = place % 256
        hot = jnp.where(iota((256, 256), 0) == within, 1.0, 0.0).astype(jnp.bfloat16)
        for q in range(CLON // 2):
            mask = jnp.where(across == q, 1.0, 0.0).astype(jnp.bfloat16)
            put = lax.dot_general(
                both * mask,
                hot,
                (((1,), (1,)), ((), ())),
                preferred_element_type=jnp.float32,
            )
            put = put[:LEV] + put[LEV:]
            state[0, 2 * q + 1] += put[:, :LANES]
            state[0, 2 * q + 2] += put[:, LANES:]

    def gather_step(t, carry):
        gather(t, True)
        return carry

    lax.fori_loop(0, DEVICES // 4 - 1, gather_step, 0)
    gather(DEVICES // 4 - 1, False)

    wide = iota((LEV, LANES), 1)

    def pack(i, value, field):
        return jnp.where(wide // 2 == i, pltpu.roll(value, 2 * i + 1, 1), field)

    edge[0] = jnp.zeros((LEV, LANES), jnp.float32)

    def pack_first(i, carry):
        edge[0] = pack(i, state[0, i + 1], edge[0])
        return carry

    lax.fori_loop(0, CLON, pack_first, 0)
    flux[...] = jnp.zeros((CLON, LANES), jnp.float32)
    pltpu.make_async_copy(wind, wind, wind_sem).wait()

    east, west = (lon + 1) % 32, (lon + 31) % 32
    north, south = (lat + 1) % 4, (lat + 3) % 4

    def edge_copies(s):
        parts = (
            (state.at[s, 1], state.at[s, CLON + 1], (west, lat)),
            (state.at[s, CLON], state.at[s, 0], (east, lat)),
            (edge.at[s], from_south.at[s], (lon, north)),
            (edge.at[s], from_north.at[s], (lon, south)),
        )
        return [
            pltpu.make_async_remote_copy(
                src_ref=source,
                dst_ref=target,
                send_sem=edge_send.at[4 * s + i],
                recv_sem=edge_recv.at[4 * s + i],
                device_id=to(*there),
            )
            for i, (source, target, there) in enumerate(parts)
        ]

    for s in range(STEPS):
        copies = edge_copies(s)
        for copy in copies:
            copy.start()
        for copy in copies:
            copy.wait_recv()
        below = jnp.where(lat > 0, from_south[s], 0.0)
        above = jnp.where(lat < 3, from_north[s], 0.0)
        halo[...] = jnp.where(wide % 2 == 0, below, pltpu.roll(above, LANES - 2, 1))
        if s + 1 < STEPS:
            edge[s + 1] = jnp.zeros((LEV, LANES), jnp.float32)

        def advance(q, carry):
            moved, inside, sources = [], [], []
            for h in range(2):
                i = 2 * q + h
                x = state[s, i + 1]
                a, b = wind[0, i], wind[1, i]
                ends = pltpu.roll(halo[...], (LANES - 2 * i) % LANES, 1)
                after = jnp.where(wide == LANES - 1, ends, pltpu.roll(x, LANES - 1, 1))
                before = jnp.where(wide == 0, ends, pltpu.roll(x, 1, 1))
                along = jnp.where(a > 0, state[s, i + 2], state[s, i])
                over = jnp.where(b > 0, after, before)
                t = x + jnp.abs(a) * (along - x) + jnp.abs(b) * (over - x)
                inner = iota((LEV, LANES), 0) < cloud_top[pl.ds(i, 1), :]
                source = jnp.where(inner, t * strength[pl.ds(i, 1), :], 0.0)
                high, rest = split(source)
                pad = jnp.zeros((DEPTH - 3 * LEV, LANES), jnp.float32)
                moved.append(t)
                inside.append(inner)
                sources.append(jnp.concatenate([high, rest, high, pad], axis=0))
            stack = jnp.concatenate(sources, axis=1).astype(jnp.bfloat16)
            mixed = jnp.dot(mixer[...], stack, preferred_element_type=jnp.float32)
            for h in range(2):
                i = 2 * q + h
                part = mixed[:, h * LANES : (h + 1) * LANES]
                value = moved[h] + jnp.where(inside[h], part, 0.0)
                state[s + 1, i + 1] = value
                flux[pl.ds(i, 1), :] += value[0:1]
                if s + 1 < STEPS:
                    edge[s + 1] = pack(i, value, edge[s + 1])
            return carry

        lax.fori_loop(0, CLON // 2, advance, 0)

    result = pltpu.make_async_copy(state.at[STEPS, pl.ds(1, CLON)], out, out_sem)
    result.start()

    def sent(k, carry):
        block_copy(k, (lon, lat)).wait_send()
        return carry

    lax.fori_loop(0, mine, sent, 0)
    block_copy(DEVICES - 1, (lon, lat)).wait_send()
    for s in range(STEPS):
        for copy in edge_copies(s):
            copy.wait_send()
    result.wait()


def on_device(
    kernels,
    weighted_residuals,
    sounding_columns,
    segment_counts,
    courant,
    mix_strength,
    cloud_top,
    redistribution,
):
    in_vmem = pl.BlockSpec(memory_space=pltpu.VMEM)
    anywhere = pl.BlockSpec(memory_space=pl.ANY)
    f32 = jnp.float32
    field, flux = pl.pallas_call(
        kernel,
        out_shape=(
            jax.ShapeDtypeStruct((CLON, LEV, LANES), f32),
            jax.ShapeDtypeStruct((CLON, LANES), f32),
        ),
        in_specs=[
            anywhere,
            in_vmem,
            in_vmem,
            pl.BlockSpec(memory_space=pltpu.SMEM),
            anywhere,
            in_vmem,
            in_vmem,
            in_vmem,
        ],
        out_specs=(anywhere, in_vmem),
        scratch_shapes=[
            pltpu.VMEM((LEV, CHIPS * LANES), f32),
            pltpu.VMEM((2, CLON, LEV, LANES), f32),
            pltpu.VMEM((DEVICES, ROWS, LANES), f32),
            pltpu.VMEM((DEVICES, ROWS, LANES), f32),
            pltpu.VMEM((STEPS + 1, CLON + 2, LEV, LANES), f32),
            pltpu.VMEM((STEPS, LEV, LANES), f32),
            pltpu.VMEM((STEPS, LEV, LANES), f32),
            pltpu.VMEM((STEPS, LEV, LANES), f32),
            pltpu.VMEM((LEV, LANES), f32),
            pltpu.VMEM((LEV, DEPTH), jnp.bfloat16),
            pltpu.SemaphoreType.DMA,
            pltpu.SemaphoreType.DMA,
            pltpu.SemaphoreType.DMA((DEVICES,)),
            pltpu.SemaphoreType.DMA((DEVICES,)),
            pltpu.SemaphoreType.DMA((4 * STEPS,)),
            pltpu.SemaphoreType.DMA((4 * STEPS,)),
            pltpu.SemaphoreType.DMA,
        ],
        compiler_params=pltpu.CompilerParams(
            collective_id=0, has_side_effects=True, vmem_limit_bytes=50 * 2**20
        ),
    )(
        kernels,
        weighted_residuals.reshape(CHIPS, LANES),
        sounding_columns.reshape(CHIPS, LANES),
        segment_counts,
        courant,
        mix_strength,
        cloud_top,
        redistribution,
    )
    return field.transpose(1, 0, 2), flux


def solution(mesh):
    return jax.shard_map(
        on_device,
        mesh=mesh,
        in_specs=(
            P(None, ("lon", "lat")),
            P(("lon", "lat")),
            P(("lon", "lat")),
            P(("lon", "lat"), None),
            P(None, None, "lon", "lat"),
            P("lon", "lat"),
            P("lon", "lat"),
            P(),
        ),
        out_specs=(P(None, "lon", "lat"), P("lon", "lat")),
        check_vma=False,
    )
```

profile of v0, /device:TPU:1, one launch (start us, length us, event | category | flops | bytes accessed | tf_op | source)
XLA Modules:
  0.0 141.1 jit_solution(5199390842833334268)
XLA Ops:
  0.6 0.0 copy-start
  0.6 0.8 copy-done
  1.4 0.0 copy-start.1
  1.4 0.8 copy-done.1
  2.2 0.0 copy-start.2
  2.2 0.8 copy-done.2
  2.9 0.0 copy-start.3
  2.9 0.7 copy-done.3
  3.7 0.0 copy-start.4
  3.7 0.7 copy-done.4
  4.4 0.0 copy-start.5
  4.4 0.7 copy-done.5
  5.0 133.9 %shard_map.95 = (f32[48,72,128]{2,1,0:T(8,128)S(1)}, f32[48,128]{1,0:T(8,128)S(1)}) custom-call(f32[72,8192]{1,0:T(8,128)} %kernels.1, f32[64,128]{1,0:T(8,128)S(1)} %bitcast.4, s32[64,128]{1,0:T(8,128)S(1)} %bitcast.5, s32[1,128]{1,0:T(1,128)S(1)} %copy-done.5, f32[2,72,48,128]{3,2,1,0:T(8,128)} %courant.1, f32[48,128]{1,0:T(8,128)S(1)} %copy-done.3, ...), custom_call_target="tpu_custom_call" | custom-call | tf_op jit(solution)/shard_map/pallas_call | solution.py:315
  138.9 1.5 %copy.10 = f32[72,48,128]{2,1,0:T(8,128)} copy(f32[72,48,128]{2,0,1:T(8,128)S(1)} %bitcast.3) | data formatting | bytes 3538944
  140.4 0.6 copy.12
Async XLA Ops:
  0.6 0.8 copy-start
  1.4 0.8 copy-start.1
  2.2 0.8 copy-start.2
  2.9 0.7 copy-start.3
  3.7 0.7 copy-start.4
  4.4 0.7 copy-start.5
where the time goes:
time: 141 us
  Pallas kernels  134 us (95%)
  local copies, waits for them, and re-layouts  6.54 us (5%)
    pallas_call x1, Pallas kernels, on_device(): pl.pallas_call(kernel, out_shape=(jax.ShapeDtypeStruct((CLON, LEV, LANES)...  134 us
    unnamed x14, local copies, waits for them, and re-layouts  6.54 us

commit v1 on v0

--- a/solution.py
+++ b/solution.py
@@ -14,6 +14,8 @@
 CHIPS = 64
 DEVICES = 128
 ROWS = 37
+BLOCKS = 8
+UNROLL = 6
 DEPTH = 224
 
 OFFSETS = sorted(
@@ -27,10 +29,19 @@
     return lon % 4, (lon // 4) % 4, (lat // 2) * 2 + lon // 16, lat % 2
 
 
-def at_offset(x, y, z, c):
-    mx, my, mz, mc = coords()
-    x, y, z, c = (mx + x) % 4, (my + y) % 4, (mz + z) % 4, (mc + c) % 2
-    return (z % 2) * 16 + y * 4 + x, (z // 2) * 2 + c
+def placer():
+    x, y, z, c = coords()
+    xs = [lax.rem(x + d, 4) for d in range(4)]
+    ys = [lax.rem(y + d, 4) * 4 for d in range(4)]
+    zs = [lax.rem(z + d, 4) for d in range(4)]
+    inner = [lax.rem(v, 2) * 16 for v in zs]
+    outer = [lax.div(v, 2) * 2 for v in zs]
+    cores = [c, 1 - c]
+
+    def place(dx, dy, dz, dc):
+        return inner[dz] + ys[dy] + xs[dx], outer[dz] + cores[dc]
+
+    return place
 
 
 def to(lon, lat):
@@ -48,20 +59,31 @@
 
 def kernel(
     kernels,
+    residuals_in,
+    columns_in,
+    counts_in,
+    courant,
+    strength_in,
+    cloud_top_in,
+    redistribution_in,
+    out,
+    flux,
     residuals,
     columns,
     counts,
-    courant,
     strength,
     cloud_top,
     redistribution,
-    out,
-    flux,
+    small_sem,
     forcing_in,
     wind,
     send,
     recv,
-    state,
+    state_0,
+    state_1,
+    state_2,
+    state_3,
+    state_4,
     edge,
     from_south,
     from_north,
@@ -75,18 +97,32 @@
     edge_recv,
     out_sem,
 ):
+    states = (state_0, state_1, state_2, state_3, state_4)
     lon, lat = lax.axis_index("lon"), lax.axis_index("lat")
     core = lat % 2
+    at_offset = placer()
     load = pltpu.make_async_copy(kernels, forcing_in, load_sem)
     load.start()
+    small = [
+        pltpu.make_async_copy(source, target, small_sem.at[i])
+        for i, (source, target) in enumerate(
+            (
+                (counts_in, counts),
+                (residuals_in, residuals),
+                (columns_in, columns),
+                (strength_in, strength),
+                (cloud_top_in, cloud_top),
+                (redistribution_in, redistribution),
+            )
+        )
+    ]
+    for copy in small:
+        copy.start()
     barrier = pltpu.get_barrier_semaphore()
-
-    def greet(k, carry):
-        there = at_offset(k % 4, (k // 4) % 4, (k // 16) % 4, k // 64)
-        pl.semaphore_signal(barrier, 1, device_id=to(*there))
-        return carry
-
-    lax.fori_loop(1, DEVICES, greet, 0)
+    for offset in OFFSETS:
+        for c in range(2):
+            if any(offset) or c:
+                pl.semaphore_signal(barrier, 1, device_id=to(*at_offset(*offset, c)))
 
     def fetch(i, carry):
         for part in range(2):
@@ -104,6 +140,8 @@
     def lo_half(shape):
         return iota(shape, 1) < 64
 
+    for copy in small:
+        copy.wait()
     load.wait()
     for m, offset in enumerate(OFFSETS):
         there_lon, there_lat = at_offset(*offset, 0)
@@ -154,7 +192,7 @@
     ).astype(jnp.bfloat16)
 
     def clear(i, carry):
-        state[0, i] = jnp.zeros((LEV, LANES), jnp.float32)
+        state_0[i] = jnp.zeros((LEV, LANES), jnp.float32)
         return carry
 
     lax.fori_loop(1, CLON + 1, clear, 0)
@@ -171,50 +209,58 @@
         return jnp.concatenate([top, bottom, end], axis=0), end_top[7:8]
 
     def gather(t, whole):
-        first = 4 * t
-        for i in range(4):
-            if whole or i != mine % 4:
+        first = BLOCKS * t
+        values, places = [], []
+        for i in range(BLOCKS):
+            if whole or i != mine % BLOCKS:
                 block_copy(first + i, (lon, lat)).wait_recv()
-        one, place_1 = paired(first)
-        two, place_2 = paired(first + 2)
-        value = jnp.concatenate([one, two], axis=1)
-        place = jnp.concatenate([place_1, place_2], axis=1).astype(jnp.int32)
-        high, rest = split(value)
-        both = jnp.concatenate([high, rest], axis=0).astype(jnp.bfloat16)
-        across = place // 256
-        within = place % 256
-        hot = jnp.where(iota((256, 256), 0) == within, 1.0, 0.0).astype(jnp.bfloat16)
-        for q in range(CLON // 2):
-            mask = jnp.where(across == q, 1.0, 0.0).astype(jnp.bfloat16)
+        for i in range(0, BLOCKS, 2):
+            value, place = paired(first + i)
+            high, rest = split(value)
+            values.append(jnp.concatenate([high, rest], axis=0))
+            places.append(place)
+        both = jnp.concatenate(values, axis=1).astype(jnp.bfloat16)
+        place = jnp.concatenate(places, axis=1).astype(jnp.int32)
+        across = lax.div(place, 256)
+        within = lax.rem(place, 256)
+        hot = iota((256, BLOCKS * 64), 0) == within
+        hot = jnp.where(hot, 1.0, 0.0).astype(jnp.bfloat16)
+        for q in range(0, CLON // 2, 2):
+            masks = [
+                jnp.where(across == q + h, 1.0, 0.0).astype(jnp.bfloat16) for h in range(2)
+            ]
             put = lax.dot_general(
-                both * mask,
+                jnp.concatenate([both * mask for mask in masks], axis=0),
                 hot,
                 (((1,), (1,)), ((), ())),
                 preferred_element_type=jnp.float32,
             )
-            put = put[:LEV] + put[LEV:]
-            state[0, 2 * q + 1] += put[:, :LANES]
-            state[0, 2 * q + 2] += put[:, LANES:]
+            for h in range(2):
+                part = put[2 * h * LEV : (2 * h + 1) * LEV]
+                part = part + put[(2 * h + 1) * LEV : (2 * h + 2) * LEV]
+                state_0[2 * (q + h) + 1] += part[:, :LANES]
+                state_0[2 * (q + h) + 2] += part[:, LANES:]
 
     def gather_step(t, carry):
         gather(t, True)
         return carry
 
-    lax.fori_loop(0, DEVICES // 4 - 1, gather_step, 0)
-    gather(DEVICES // 4 - 1, False)
+    lax.fori_loop(0, DEVICES // BLOCKS - 1, gather_step, 0)
+    gather(DEVICES // BLOCKS - 1, False)
 
     wide = iota((LEV, LANES), 1)
 
     def pack(i, value, field):
         return jnp.where(wide // 2 == i, pltpu.roll(value, 2 * i + 1, 1), field)
 
-    edge[0] = jnp.zeros((LEV, LANES), jnp.float32)
-
-    def pack_first(i, carry):
-        edge[0] = pack(i, state[0, i + 1], edge[0])
-        return carry
-
-    lax.fori_loop(0, CLON, pack_first, 0)
+    def pack_first(g, field):
+        for k in range(UNROLL):
+            i = g * UNROLL + k
+            field = pack(i, state_0[i + 1], field)
+        return field
+
+    nothing = jnp.zeros((LEV, LANES), jnp.float32)
+    edge[0] = lax.fori_loop(0, CLON // UNROLL, pack_first, nothing)
     flux[...] = jnp.zeros((CLON, LANES), jnp.float32)
     pltpu.make_async_copy(wind, wind, wind_sem).wait()
 
@@ -223,8 +269,8 @@
 
     def edge_copies(s):
         parts = (
-            (state.at[s, 1], state.at[s, CLON + 1], (west, lat)),
-            (state.at[s, CLON], state.at[s, 0], (east, lat)),
+            (states[s].at[1], states[s].at[CLON + 1], (west, lat)),
+            (states[s].at[CLON], states[s].at[0], (east, lat)),
             (edge.at[s], from_south.at[s], (lon, north)),
             (edge.at[s], from_north.at[s], (lon, south)),
         )
@@ -248,43 +294,46 @@
         below = jnp.where(lat > 0, from_south[s], 0.0)
         above = jnp.where(lat < 3, from_north[s], 0.0)
         halo[...] = jnp.where(wide % 2 == 0, below, pltpu.roll(above, LANES - 2, 1))
+        now, later = states[s], states[s + 1]
+
+        def advance(g, field):
+            for k in range(UNROLL):
+                moved, inside, sources = [], [], []
+                for h in range(2):
+                    i = 2 * (g * UNROLL + k) + h
+                    x = now[i + 1]
+                    a, b = wind[0, i], wind[1, i]
+                    ends = pltpu.roll(halo[...], lax.rem(LANES - 2 * i, LANES), 1)
+                    after = pltpu.roll(x, LANES - 1, 1)
+                    after = jnp.where(wide == LANES - 1, ends, after)
+                    before = jnp.where(wide == 0, ends, pltpu.roll(x, 1, 1))
+                    along = jnp.where(a > 0, now[i + 2], now[i])
+                    over = jnp.where(b > 0, after, before)
+                    t = x + jnp.abs(a) * (along - x) + jnp.abs(b) * (over - x)
+                    inner = iota((LEV, LANES), 0) < cloud_top[pl.ds(i, 1), :]
+                    source = jnp.where(inner, t * strength[pl.ds(i, 1), :], 0.0)
+                    high, rest = split(source)
+                    pad = jnp.zeros((DEPTH - 3 * LEV, LANES), jnp.float32)
+                    moved.append(t)
+                    inside.append(inner)
+                    sources.append(jnp.concatenate([high, rest, high, pad], axis=0))
+                stack = jnp.concatenate(sources, axis=1).astype(jnp.bfloat16)
+                mixed = jnp.dot(mixer[...], stack, preferred_element_type=jnp.float32)
+                for h in range(2):
+                    i = 2 * (g * UNROLL + k) + h
+                    part = mixed[:, h * LANES : (h + 1) * LANES]
+                    value = moved[h] + jnp.where(inside[h], part, 0.0)
+                    later[i + 1] = value
+                    flux[pl.ds(i, 1), :] += value[0:1]
+                    if s + 1 < STEPS:
+                        field = pack(i, value, field)
+            return field
+
+        packed = lax.fori_loop(0, CLON // 2 // UNROLL, advance, nothing)
         if s + 1 < STEPS:
-            edge[s + 1] = jnp.zeros((LEV, LANES), jnp.float32)
-
-        def advance(q, carry):
-            moved, inside, sources = [], [], []
-            for h in range(2):
-                i = 2 * q + h
-                x = state[s, i + 1]
-                a, b = wind[0, i], wind[1, i]
-                ends = pltpu.roll(halo[...], (LANES - 2 * i) % LANES, 1)
-                after = jnp.where(wide == LANES - 1, ends, pltpu.roll(x, LANES - 1, 1))
-                before = jnp.where(wide == 0, ends, pltpu.roll(x, 1, 1))
-                along = jnp.where(a > 0, state[s, i + 2], state[s, i])
-                over = jnp.where(b > 0, after, before)
-                t = x + jnp.abs(a) * (along - x) + jnp.abs(b) * (over - x)
-                inner = iota((LEV, LANES), 0) < cloud_top[pl.ds(i, 1), :]
-                source = jnp.where(inner, t * strength[pl.ds(i, 1), :], 0.0)
-                high, rest = split(source)
-                pad = jnp.zeros((DEPTH - 3 * LEV, LANES), jnp.float32)
-                moved.append(t)
-                inside.append(inner)
-                sources.append(jnp.concatenate([high, rest, high, pad], axis=0))
-            stack = jnp.concatenate(sources, axis=1).astype(jnp.bfloat16)
-            mixed = jnp.dot(mixer[...], stack, preferred_element_type=jnp.float32)
-            for h in range(2):
-                i = 2 * q + h
-                part = mixed[:, h * LANES : (h + 1) * LANES]
-                value = moved[h] + jnp.where(inside[h], part, 0.0)
-                state[s + 1, i + 1] = value
-                flux[pl.ds(i, 1), :] += value[0:1]
-                if s + 1 < STEPS:
-                    edge[s + 1] = pack(i, value, edge[s + 1])
-            return carry
-
-        lax.fori_loop(0, CLON // 2, advance, 0)
-
-    result = pltpu.make_async_copy(state.at[STEPS, pl.ds(1, CLON)], out, out_sem)
+            edge[s + 1] = packed
+
+    result = pltpu.make_async_copy(state_4.at[pl.ds(1, CLON)], out, out_sem)
     result.start()
 
     def sent(k, carry):
@@ -318,23 +367,21 @@
             jax.ShapeDtypeStruct((CLON, LEV, LANES), f32),
             jax.ShapeDtypeStruct((CLON, LANES), f32),
         ),
-        in_specs=[
-            anywhere,
-            in_vmem,
-            in_vmem,
-            pl.BlockSpec(memory_space=pltpu.SMEM),
-            anywhere,
-            in_vmem,
-            in_vmem,
-            in_vmem,
-        ],
+        in_specs=[pl.BlockSpec(memory_space=pltpu.HBM)] * 8,
         out_specs=(anywhere, in_vmem),
         scratch_shapes=[
+            pltpu.VMEM((CHIPS, LANES), f32),
+            pltpu.VMEM((CHIPS, LANES), jnp.int32),
+            pltpu.SMEM((1, DEVICES), jnp.int32),
+            pltpu.VMEM((CLON, LANES), f32),
+            pltpu.VMEM((CLON, LANES), jnp.int32),
+            pltpu.VMEM((LEV, LEV), f32),
+            pltpu.SemaphoreType.DMA((6,)),
             pltpu.VMEM((LEV, CHIPS * LANES), f32),
             pltpu.VMEM((2, CLON, LEV, LANES), f32),
             pltpu.VMEM((DEVICES, ROWS, LANES), f32),
             pltpu.VMEM((DEVICES, ROWS, LANES), f32),
-            pltpu.VMEM((STEPS + 1, CLON + 2, LEV, LANES), f32),
+            *[pltpu.VMEM((CLON + 2, LEV, LANES), f32) for _ in range(STEPS + 1)],
             pltpu.VMEM((STEPS, LEV, LANES), f32),
             pltpu.VMEM((STEPS, LEV, LANES), f32),
             pltpu.VMEM((STEPS, LEV, LANES), f32),
@@ -349,7 +396,7 @@
             pltpu.SemaphoreType.DMA,
         ],
         compiler_params=pltpu.CompilerParams(
-            collective_id=0, has_side_effects=True, vmem_limit_bytes=50 * 2**20
+            collective_id=0, has_side_effects=True, vmem_limit_bytes=60 * 2**20
         ),
     )(
         kernels,

time: 141 us -> 92.9 us (0.66)
  Pallas kernels: 134 us -> 88.4 us
  local copies, waits for them, and re-layouts: 6.54 us -> 3.64 us
    pallas_call x1, Pallas kernels: 134 us -> 88.4 us  [on_device(): pl.pallas_call(kernel, out_shape=(jax.ShapeDtypeStruct((CLON, LEV, LANES)...]
    unnamed x14 -> x4, local copies, waits for them, and re-layouts: 6.54 us -> 3.64 us
where the time goes in v1:
time: 92.9 us; the launch traced here: 92.7 us
  Pallas kernels  88.4 us (95%)
  local copies, waits for them, and re-layouts  3.64 us (4%)
    pallas_call x1, Pallas kernels, on_device(): pl.pallas_call(kernel, out_shape=(jax.ShapeDtypeStruct((CLON, LEV, LANES)...  88.4 us
    unnamed x4, local copies, waits for them, and re-layouts  3.64 us

profile of v1, /device:TPU:1, one launch (start us, length us, event | category | flops | bytes accessed | tf_op | source)
XLA Modules:
  0.0 92.7 jit_solution(8694908427472403781)
XLA Ops:
  0.6 88.4 %shard_map.95 = (f32[48,72,128]{2,1,0:T(8,128)}, f32[48,128]{1,0:T(8,128)}) custom-call(f32[72,8192]{1,0:T(8,128)} %kernels.1, f32[64,128]{1,0:T(8,128)} %bitcast.4, s32[64,128]{1,0:T(8,128)} %bitcast.5, s32[1,128]{1,0:T(1,128)} %counts_in.1, f32[2,72,48,128]{3,2,1,0:T(8,128)} %courant.1, f32[48,128]{1,0:T(8,128)} %strength_in.1, s32[48,128]{1,0:T(8,128)} %cloud_top_in.1, ...), custom_call_target="tpu_custom_call" | custom-call | tf_op jit(solution)/shard_map/pallas_call | solution.py:364
  89.1 0.0 copy-start
  89.1 3.0 %copy.10 = f32[72,48,128]{2,1,0:T(8,128)} copy(f32[72,48,128]{2,0,1:T(8,128)} %bitcast.3) | data formatting | bytes 3538944
  92.1 0.0 copy-done
  92.1 0.6 copy.12
Async XLA Ops:
  89.1 3.0 %copy-start = (f32[48,128]{1,0:T(8,128)S(1)}, f32[48,128]{1,0:T(8,128)}, u32[]{:S(2)}) copy-start(f32[48,128]{1,0:T(8,128)} %get-tuple-element.11) | copy-start | bytes 73732

commit v2 on v1

--- a/solution.py
+++ b/solution.py
@@ -16,11 +16,15 @@
 ROWS = 37
 BLOCKS = 8
 UNROLL = 6
+PAIRS = 11
+FIRST = 64
+GROUP = 16
 DEPTH = 224
 
 OFFSETS = sorted(
-    itertools.product(range(4), repeat=3), key=lambda o: -sum(min(v, 4 - v) for v in o)
+    itertools.product(range(4), repeat=3), key=lambda o: sum(min(v, 4 - v) for v in o)
 )
+OFFSETS = OFFSETS[1:] + OFFSETS[:1]
 
 
 def coords():
@@ -55,6 +59,46 @@
 def split(value):
     high = value.astype(jnp.bfloat16).astype(jnp.float32)
     return high, value - high
+
+
+def lanes(low, high):
+    lane = iota((1, LANES), 1)
+    return (lane == low) | (lane == high)
+
+
+def pack_ends(i, value, field):
+    return jnp.where(lanes(2 * i, 2 * i + 1), pltpu.roll(value, 2 * i + 1, 1), field)
+
+
+def pack_near(i, value, field):
+    return jnp.where(lanes(2 * i, 2 * i + 3), pltpu.roll(value, 2 * i + 2, 1), field)
+
+
+def put_ends(i, field, value):
+    ends = pltpu.roll(field, LANES - 1 - 2 * i, 1)
+    return jnp.where(lanes(LANES - 1, 0), ends, value)
+
+
+def transport(x, east, west, north, south, a, b):
+    along = jnp.where(a > 0, east, west)
+    over = jnp.where(b > 0, north, south)
+    return x + jnp.abs(a) * (along - x) + jnp.abs(b) * (over - x)
+
+
+def convect(columns, mixer):
+    sources, inside = [], []
+    for field, top, strength in columns:
+        inner = iota((LEV, LANES), 0) < top
+        high, rest = split(jnp.where(inner, field * strength, 0.0))
+        pad = jnp.zeros((DEPTH - 3 * LEV, LANES), jnp.float32)
+        sources.append(jnp.concatenate([high, rest, high, pad], axis=0))
+        inside.append(inner)
+    stack = jnp.concatenate(sources, axis=1).astype(jnp.bfloat16)
+    mixed = jnp.dot(mixer, stack, preferred_element_type=jnp.float32)
+    return [
+        column[0] + jnp.where(inner, mixed[:, h * LANES : (h + 1) * LANES], 0.0)
+        for h, (column, inner) in enumerate(zip(columns, inside))
+    ]
 
 
 def kernel(
@@ -87,7 +131,9 @@
     edge,
     from_south,
     from_north,
-    halo,
+    strip_wind,
+    strip_strength,
+    strip_top,
     mixer,
     load_sem,
     wind_sem,
@@ -95,14 +141,20 @@
     recv_sem,
     edge_send,
     edge_recv,
-    out_sem,
 ):
     states = (state_0, state_1, state_2, state_3, state_4)
     lon, lat = lax.axis_index("lon"), lax.axis_index("lat")
     core = lat % 2
     at_offset = placer()
-    load = pltpu.make_async_copy(kernels, forcing_in, load_sem)
-    load.start()
+    chips = [at_offset(*offset, 0) for offset in OFFSETS]
+    chips = [there_lon * 2 + lax.div(there_lat, 2) for there_lon, there_lat in chips]
+
+    def load(m):
+        at = pl.ds(pl.multiple_of(chips[m] * LANES, LANES), LANES)
+        return pltpu.make_async_copy(
+            kernels.at[:, at], forcing_in.at[:, at], load_sem.at[m]
+        )
+
     small = [
         pltpu.make_async_copy(source, target, small_sem.at[i])
         for i, (source, target) in enumerate(
@@ -118,6 +170,8 @@
     ]
     for copy in small:
         copy.start()
+    for m in range(CHIPS):
+        load(m).start()
     barrier = pltpu.get_barrier_semaphore()
     for offset in OFFSETS:
         for c in range(2):
@@ -140,12 +194,20 @@
     def lo_half(shape):
         return iota(shape, 1) < 64
 
-    for copy in small:
-        copy.wait()
-    load.wait()
-    for m, offset in enumerate(OFFSETS):
-        there_lon, there_lat = at_offset(*offset, 0)
-        chip = there_lon * 2 + there_lat // 2
+    def block_copy(k, there):
+        return pltpu.make_async_remote_copy(
+            src_ref=send.at[k],
+            dst_ref=recv.at[k],
+            send_sem=send_sem.at[k],
+            recv_sem=recv_sem.at[k],
+            device_id=to(*there),
+        )
+
+    mine = DEVICES - 2
+
+    def send_to(m):
+        load(m).wait()
+        chip = chips[m]
         one = counts[0, 2 * chip]
         two = counts[0, 2 * chip + 1]
         row = iota((1, LANES), 1)
@@ -168,23 +230,17 @@
         send[slot_1, 0:32, :] = jnp.where(half, pltpu.roll(a, 64, 1), b)
         send[slot_0, 32:ROWS, :] = tail_0[0:5]
         send[slot_1, 32:ROWS, :] = tail_1[0:5]
-    mine = DEVICES - 2
-    recv[mine] = send[mine]
-
-    def block_copy(k, there):
-        return pltpu.make_async_remote_copy(
-            src_ref=send.at[k],
-            dst_ref=recv.at[k],
-            send_sem=send_sem.at[k],
-            recv_sem=recv_sem.at[k],
-            device_id=to(*there),
-        )
-
-    pl.semaphore_wait(barrier, DEVICES - 1)
-    for m, offset in enumerate(OFFSETS):
         for c in range(2):
             if 2 * m + c != mine:
-                block_copy(2 * m + c, at_offset(*offset, c)).start()
+                block_copy(2 * m + c, at_offset(*OFFSETS[m], c)).start()
+            else:
+                recv[mine] = send[mine]
+
+    for copy in small:
+        copy.wait()
+    pl.semaphore_wait(barrier, DEVICES - 1)
+    for m in range(FIRST):
+        send_to(m)
 
     high, rest = split(redistribution[...].T)
     mixer[...] = jnp.concatenate(
@@ -196,6 +252,26 @@
         return carry
 
     lax.fori_loop(1, CLON + 1, clear, 0)
+
+    pltpu.make_async_copy(wind, wind, wind_sem).wait()
+    nothing = jnp.zeros((LEV, LANES), jnp.float32)
+    few = jnp.zeros((8, LANES), jnp.float32)
+
+    def pack_static(g, fields):
+        a, b, c, d = fields
+        for k in range(UNROLL):
+            i = g * UNROLL + k
+            a = pack_ends(i, wind[0, i], a)
+            b = pack_ends(i, wind[1, i], b)
+            row = strength[pl.ds(i, 1), :]
+            c = pack_ends(i, jnp.broadcast_to(row, (8, LANES)), c)
+            row = cloud_top[pl.ds(i, 1), :].astype(jnp.float32)
+            d = pack_ends(i, jnp.broadcast_to(row, (8, LANES)), d)
+        return a, b, c, d
+
+    strips = lax.fori_loop(0, CLON // UNROLL, pack_static, (nothing, nothing, few, few))
+    strip_wind[0], strip_wind[1], strip_strength[...] = strips[:3]
+    strip_top[...] = strips[3].astype(jnp.int32)
 
     def paired(k):
         half = lo_half((32, LANES))
@@ -245,34 +321,37 @@
         gather(t, True)
         return carry
 
-    lax.fori_loop(0, DEVICES // BLOCKS - 1, gather_step, 0)
+    ahead = FIRST
+    for t in range(0, DEVICES // BLOCKS, GROUP):
+        whole = t + GROUP < DEVICES // BLOCKS
+        lax.fori_loop(t, t + GROUP - (0 if whole else 1), gather_step, 0)
+        for m in range(ahead, min(ahead + GROUP * BLOCKS // 2, CHIPS)):
+            send_to(m)
+        ahead += GROUP * BLOCKS // 2
     gather(DEVICES // BLOCKS - 1, False)
 
-    wide = iota((LEV, LANES), 1)
-
-    def pack(i, value, field):
-        return jnp.where(wide // 2 == i, pltpu.roll(value, 2 * i + 1, 1), field)
-
-    def pack_first(g, field):
+    def pack_first(g, fields):
+        ends, near = fields
         for k in range(UNROLL):
             i = g * UNROLL + k
-            field = pack(i, state_0[i + 1], field)
-        return field
-
-    nothing = jnp.zeros((LEV, LANES), jnp.float32)
-    edge[0] = lax.fori_loop(0, CLON // UNROLL, pack_first, nothing)
+            value = state_0[i + 1]
+            ends, near = pack_ends(i, value, ends), pack_near(i, value, near)
+        return ends, near
+
+    first = lax.fori_loop(0, CLON // UNROLL, pack_first, (nothing, nothing))
+    edge[0], near = first
     flux[...] = jnp.zeros((CLON, LANES), jnp.float32)
-    pltpu.make_async_copy(wind, wind, wind_sem).wait()
-
-    east, west = (lon + 1) % 32, (lon + 31) % 32
-    north, south = (lat + 1) % 4, (lat + 3) % 4
+    flux_ends = few
+
+    east, west = lax.rem(lon + 1, 32), lax.rem(lon + 31, 32)
+    north, south = lax.rem(lat + 1, 4), lax.rem(lat + 3, 4)
 
     def edge_copies(s):
         parts = (
+            (edge.at[s], from_south.at[s], (lon, north)),
+            (edge.at[s], from_north.at[s], (lon, south)),
             (states[s].at[1], states[s].at[CLON + 1], (west, lat)),
             (states[s].at[CLON], states[s].at[0], (east, lat)),
-            (edge.at[s], from_south.at[s], (lon, north)),
-            (edge.at[s], from_north.at[s], (lon, south)),
         )
         return [
             pltpu.make_async_remote_copy(
@@ -285,56 +364,77 @@
             for i, (source, target, there) in enumerate(parts)
         ]
 
+    even = lax.rem(iota((1, LANES), 1), 2) == 0
+
     for s in range(STEPS):
-        copies = edge_copies(s)
-        for copy in copies:
+        now, later = states[s], states[s + 1]
+        for copy in edge_copies(s):
             copy.start()
-        for copy in copies:
+
+        def row(i, ends):
+            x = now[i + 1] if ends is None else put_ends(i, ends, now[i + 1])
+            after, before = pltpu.roll(x, LANES - 1, 1), pltpu.roll(x, 1, 1)
+            moved = transport(
+                x, now[i + 2], now[i], after, before, wind[0, i], wind[1, i]
+            )
+            return moved, cloud_top[pl.ds(i, 1), :], strength[pl.ds(i, 1), :]
+
+        def advance_pair(i, field):
+            ends = edge[s] if s else None
+            values = convect([row(i, ends), row(i + 1, ends)], mixer[...])
+            for h, value in enumerate(values):
+                later[i + h + 1] = value
+                flux[pl.ds(i + h, 1), :] += value[0:1]
+                field = pack_near(i + h, value, field)
+            return field
+
+        def advance(g, field):
+            for k in range(PAIRS):
+                field = advance_pair(1 + 2 * (g * PAIRS + k), field)
+            return field
+
+        groups = (CLON - 2) // 2 // PAIRS
+        next_near = lax.fori_loop(0, groups, advance, nothing)
+        for i in range(1 + 2 * groups * PAIRS, CLON - 1, 2):
+            next_near = advance_pair(i, next_near)
+
+        for copy in edge_copies(s):
             copy.wait_recv()
+        x = edge[s]
+        near = jnp.where(even, near, pltpu.roll(near, LANES - 2, 1))
+        above = jnp.where(lat < 3, from_north[s], 0.0)
         below = jnp.where(lat > 0, from_south[s], 0.0)
-        above = jnp.where(lat < 3, from_north[s], 0.0)
-        halo[...] = jnp.where(wide % 2 == 0, below, pltpu.roll(above, LANES - 2, 1))
-        now, later = states[s], states[s + 1]
-
-        def advance(g, field):
-            for k in range(UNROLL):
-                moved, inside, sources = [], [], []
-                for h in range(2):
-                    i = 2 * (g * UNROLL + k) + h
-                    x = now[i + 1]
-                    a, b = wind[0, i], wind[1, i]
-                    ends = pltpu.roll(halo[...], lax.rem(LANES - 2 * i, LANES), 1)
-                    after = pltpu.roll(x, LANES - 1, 1)
-                    after = jnp.where(wide == LANES - 1, ends, after)
-                    before = jnp.where(wide == 0, ends, pltpu.roll(x, 1, 1))
-                    along = jnp.where(a > 0, now[i + 2], now[i])
-                    over = jnp.where(b > 0, after, before)
-                    t = x + jnp.abs(a) * (along - x) + jnp.abs(b) * (over - x)
-                    inner = iota((LEV, LANES), 0) < cloud_top[pl.ds(i, 1), :]
-                    source = jnp.where(inner, t * strength[pl.ds(i, 1), :], 0.0)
-                    high, rest = split(source)
-                    pad = jnp.zeros((DEPTH - 3 * LEV, LANES), jnp.float32)
-                    moved.append(t)
-                    inside.append(inner)
-                    sources.append(jnp.concatenate([high, rest, high, pad], axis=0))
-                stack = jnp.concatenate(sources, axis=1).astype(jnp.bfloat16)
-                mixed = jnp.dot(mixer[...], stack, preferred_element_type=jnp.float32)
-                for h in range(2):
-                    i = 2 * (g * UNROLL + k) + h
-                    part = mixed[:, h * LANES : (h + 1) * LANES]
-                    value = moved[h] + jnp.where(inside[h], part, 0.0)
-                    later[i + 1] = value
-                    flux[pl.ds(i, 1), :] += value[0:1]
-                    if s + 1 < STEPS:
-                        field = pack(i, value, field)
-            return field
-
-        packed = lax.fori_loop(0, CLON // 2 // UNROLL, advance, nothing)
-        if s + 1 < STEPS:
-            edge[s + 1] = packed
-
-    result = pltpu.make_async_copy(state_4.at[pl.ds(1, CLON)], out, out_sem)
-    result.start()
+        after = jnp.where(even, pltpu.roll(above, LANES - 1, 1), near)
+        before = jnp.where(even, near, pltpu.roll(below, 1, 1))
+        around = pack_ends(CLON, now[CLON + 1], pack_ends(63, now[0], x))
+        moved = transport(
+            x,
+            pltpu.roll(around, LANES - 2, 1),
+            pltpu.roll(around, 2, 1),
+            after,
+            before,
+            strip_wind[0],
+            strip_wind[1],
+        )
+        strip = (moved, strip_top[0:1, :], strip_strength[0:1, :])
+        ends, one, two = convect([strip, row(0, None), row(CLON - 1, None)], mixer[...])
+        edge[s + 1] = ends
+        flux_ends = flux_ends + ends[0:8]
+        for i, value in ((0, one), (CLON - 1, two)):
+            later[i + 1] = put_ends(i, ends, value)
+            flux[pl.ds(i, 1), :] += value[0:1]
+            next_near = pack_near(i, value, next_near)
+        near = next_near
+
+    def finish(g, carry):
+        for k in range(UNROLL):
+            i = g * UNROLL + k
+            out[i] = put_ends(i, edge[STEPS], state_4[i + 1])
+            total = jnp.broadcast_to(flux[pl.ds(i, 1), :], (8, LANES))
+            flux[pl.ds(i, 1), :] = put_ends(i, flux_ends, total)[0:1]
+        return carry
+
+    lax.fori_loop(0, CLON // UNROLL, finish, 0)
 
     def sent(k, carry):
         block_copy(k, (lon, lat)).wait_send()
@@ -345,7 +445,6 @@
     for s in range(STEPS):
         for copy in edge_copies(s):
             copy.wait_send()
-    result.wait()
 
 
 def on_device(
@@ -359,16 +458,15 @@
     redistribution,
 ):
     in_vmem = pl.BlockSpec(memory_space=pltpu.VMEM)
-    anywhere = pl.BlockSpec(memory_space=pl.ANY)
     f32 = jnp.float32
     field, flux = pl.pallas_call(
         kernel,
         out_shape=(
-            jax.ShapeDtypeStruct((CLON, LEV, LANES), f32),
-            jax.ShapeDtypeStruct((CLON, LANES), f32),
+            pltpu.VMEM((CLON, LEV, LANES), f32),
+            pltpu.VMEM((CLON, LANES), f32),
         ),
-        in_specs=[pl.BlockSpec(memory_space=pltpu.HBM)] * 8,
-        out_specs=(anywhere, in_vmem),
+        in_specs=[pl.BlockSpec(memory_space=pl.ANY)] * 8,
+        out_specs=(in_vmem, in_vmem),
         scratch_shapes=[
             pltpu.VMEM((CHIPS, LANES), f32),
             pltpu.VMEM((CHIPS, LANES), jnp.int32),
@@ -382,31 +480,37 @@
             pltpu.VMEM((DEVICES, ROWS, LANES), f32),
             pltpu.VMEM((DEVICES, ROWS, LANES), f32),
             *[pltpu.VMEM((CLON + 2, LEV, LANES), f32) for _ in range(STEPS + 1)],
+            pltpu.VMEM((STEPS + 1, LEV, LANES), f32),
             pltpu.VMEM((STEPS, LEV, LANES), f32),
             pltpu.VMEM((STEPS, LEV, LANES), f32),
-            pltpu.VMEM((STEPS, LEV, LANES), f32),
-            pltpu.VMEM((LEV, LANES), f32),
+            pltpu.VMEM((2, LEV, LANES), f32),
+            pltpu.VMEM((8, LANES), f32),
+            pltpu.VMEM((8, LANES), jnp.int32),
             pltpu.VMEM((LEV, DEPTH), jnp.bfloat16),
-            pltpu.SemaphoreType.DMA,
+            pltpu.SemaphoreType.DMA((CHIPS,)),
             pltpu.SemaphoreType.DMA,
             pltpu.SemaphoreType.DMA((DEVICES,)),
             pltpu.SemaphoreType.DMA((DEVICES,)),
             pltpu.SemaphoreType.DMA((4 * STEPS,)),
             pltpu.SemaphoreType.DMA((4 * STEPS,)),
-            pltpu.SemaphoreType.DMA,
         ],
         compiler_params=pltpu.CompilerParams(
-            collective_id=0, has_side_effects=True, vmem_limit_bytes=60 * 2**20
+            collective_id=0, has_side_effects=True, vmem_limit_bytes=44 * 2**20
         ),
     )(
-        kernels,
-        weighted_residuals.reshape(CHIPS, LANES),
-        sounding_columns.reshape(CHIPS, LANES),
-        segment_counts,
-        courant,
-        mix_strength,
-        cloud_top,
-        redistribution,
+        *(
+            pltpu.with_memory_space_constraint(value, pltpu.HBM)
+            for value in (
+                kernels,
+                weighted_residuals.reshape(CHIPS, LANES),
+                sounding_columns.reshape(CHIPS, LANES),
+                segment_counts,
+                courant,
+                mix_strength,
+                cloud_top,
+                redistribution,
+            )
+        )
     )
     return field.transpose(1, 0, 2), flux
 

time: 92.9 us -> 76.3 us (0.82)
  Pallas kernels: 88.4 us -> 73.4 us
  local copies, waits for them, and re-layouts: 3.64 us -> 2.13 us
    pallas_call x1, Pallas kernels: 88.4 us -> 73.4 us  [on_device(): pl.pallas_call(kernel, out_shape=(pltpu.VMEM((CLON, LEV, LANES), f32), pl...]
    unnamed x4 -> x2, local copies, waits for them, and re-layouts: 3.64 us -> 2.13 us
where the time goes in v2:
time: 76.3 us; the launch traced here: 76.2 us
  Pallas kernels  73.4 us (96%)
  local copies, waits for them, and re-layouts  2.13 us (3%)
    pallas_call x1, Pallas kernels, on_device(): pl.pallas_call(kernel, out_shape=(pltpu.VMEM((CLON, LEV, LANES), f32), pl...  73.4 us
    unnamed x2, local copies, waits for them, and re-layouts  2.13 us

profile of v2, /device:TPU:1, one launch (start us, length us, event | category | flops | bytes accessed | tf_op | source)
XLA Modules:
  0.0 76.2 jit_solution(5414064549540415429)
XLA Ops:
  0.6 73.4 %shard_map.95 = (f32[48,72,128]{2,1,0:T(8,128)S(1)}, f32[48,128]{1,0:T(8,128)S(1)}) custom-call(f32[72,8192]{1,0:T(8,128)} %kernels.1, f32[64,128]{1,0:T(8,128)} %bitcast.4, s32[64,128]{1,0:T(8,128)} %bitcast.5, s32[1,128]{1,0:T(1,128)} %counts_in.1, f32[2,72,48,128]{3,2,1,0:T(8,128)} %courant.1, f32[48,128]{1,0:T(8,128)} %strength_in.1, ...), custom_call_target="tpu_custom_call" | custom-call | tf_op jit(solution)/shard_map/pallas_call | solution.py:462
  74.1 1.5 %copy.10 = f32[72,48,128]{2,1,0:T(8,128)} copy(f32[72,48,128]{2,0,1:T(8,128)S(1)} %bitcast.3) | data formatting | bytes 3538944
  75.6 0.6 copy.12

commit v3 on v2

--- a/solution.py
+++ b/solution.py
@@ -1,4 +1,5 @@
 import itertools
+import random
 
 import jax
 import jax.numpy as jnp
@@ -17,13 +18,12 @@
 BLOCKS = 8
 UNROLL = 6
 PAIRS = 11
-FIRST = 64
-GROUP = 16
-DEPTH = 224
-
-OFFSETS = sorted(
-    itertools.product(range(4), repeat=3), key=lambda o: sum(min(v, 4 - v) for v in o)
-)
+LAST = 4
+DEPTH = 80
+
+OFFSETS = list(itertools.product(range(4), repeat=3))
+random.Random(1).shuffle(OFFSETS)
+OFFSETS.sort(key=lambda o: sum(min(v, 4 - v) for v in o))
 OFFSETS = OFFSETS[1:] + OFFSETS[:1]
 
 
@@ -35,9 +35,10 @@
 
 def placer():
     x, y, z, c = coords()
-    xs = [lax.rem(x + d, 4) for d in range(4)]
-    ys = [lax.rem(y + d, 4) * 4 for d in range(4)]
-    zs = [lax.rem(z + d, 4) for d in range(4)]
+    way = 1 + 2 * c
+    xs = [lax.rem(x + d * way, 4) for d in range(4)]
+    ys = [lax.rem(y + d * way, 4) * 4 for d in range(4)]
+    zs = [lax.rem(z + d * way, 4) for d in range(4)]
     inner = [lax.rem(v, 2) * 16 for v in zs]
     outer = [lax.div(v, 2) * 2 for v in zs]
     cores = [c, 1 - c]
@@ -77,6 +78,11 @@
 def put_ends(i, field, value):
     ends = pltpu.roll(field, LANES - 1 - 2 * i, 1)
     return jnp.where(lanes(LANES - 1, 0), ends, value)
+
+
+def spread_ends(field):
+    even = lax.rem(iota((1, LANES), 1), 2) == 0
+    return jnp.where(even, field, pltpu.roll(field, 2, 1))
 
 
 def transport(x, east, west, north, south, a, b):
@@ -89,11 +95,14 @@
     sources, inside = [], []
     for field, top, strength in columns:
         inner = iota((LEV, LANES), 0) < top
-        high, rest = split(jnp.where(inner, field * strength, 0.0))
-        pad = jnp.zeros((DEPTH - 3 * LEV, LANES), jnp.float32)
-        sources.append(jnp.concatenate([high, rest, high, pad], axis=0))
+        source = jnp.where(inner, field * strength, 0.0)
+        pad = jnp.zeros((DEPTH - LEV, LANES), jnp.float32)
+        source = jnp.concatenate([source, pad], axis=0)
+        high = source.astype(jnp.bfloat16)
+        rest = (source - high.astype(jnp.float32)).astype(jnp.bfloat16)
+        sources.append(jnp.concatenate([high, rest, high], axis=0))
         inside.append(inner)
-    stack = jnp.concatenate(sources, axis=1).astype(jnp.bfloat16)
+    stack = jnp.concatenate(sources, axis=1)
     mixed = jnp.dot(mixer, stack, preferred_element_type=jnp.float32)
     return [
         column[0] + jnp.where(inner, mixed[:, h * LANES : (h + 1) * LANES], 0.0)
@@ -135,6 +144,7 @@
     strip_strength,
     strip_top,
     mixer,
+    spread,
     load_sem,
     wind_sem,
     send_sem,
@@ -146,6 +156,12 @@
     lon, lat = lax.axis_index("lon"), lax.axis_index("lat")
     core = lat % 2
     at_offset = placer()
+    barrier = pltpu.get_barrier_semaphore()
+    for offset in reversed(OFFSETS):
+        for c in range(2):
+            if any(offset) or c:
+                pl.semaphore_signal(barrier, 1, device_id=to(*at_offset(*offset, c)))
+
     chips = [at_offset(*offset, 0) for offset in OFFSETS]
     chips = [there_lon * 2 + lax.div(there_lat, 2) for there_lon, there_lat in chips]
 
@@ -172,12 +188,6 @@
         copy.start()
     for m in range(CHIPS):
         load(m).start()
-    barrier = pltpu.get_barrier_semaphore()
-    for offset in OFFSETS:
-        for c in range(2):
-            if any(offset) or c:
-                pl.semaphore_signal(barrier, 1, device_id=to(*at_offset(*offset, c)))
-
     def fetch(i, carry):
         for part in range(2):
             pltpu.make_async_copy(
@@ -185,7 +195,6 @@
             ).start()
         return carry
 
-    lax.fori_loop(0, CLON, fetch, 0)
 
     lane = iota((8, LANES), 1)
     sub = iota((8, LANES), 0)
@@ -239,13 +248,15 @@
     for copy in small:
         copy.wait()
     pl.semaphore_wait(barrier, DEVICES - 1)
-    for m in range(FIRST):
+    for m in range(CHIPS):
         send_to(m)
+    lax.fori_loop(0, CLON, fetch, 0)
 
     high, rest = split(redistribution[...].T)
-    mixer[...] = jnp.concatenate(
-        [high, high, rest, jnp.zeros((LEV, DEPTH - 3 * LEV), jnp.float32)], axis=1
-    ).astype(jnp.bfloat16)
+    pad = jnp.zeros((LEV, DEPTH - LEV), jnp.float32)
+    mixer[...] = jnp.concatenate([high, pad, high, pad, rest, pad], axis=1).astype(
+        jnp.bfloat16
+    )
 
     def clear(i, carry):
         state_0[i] = jnp.zeros((LEV, LANES), jnp.float32)
@@ -284,13 +295,12 @@
         end = jnp.where(sub < 4, pltpu.roll(end_top, 5, 0), pltpu.roll(end_bottom, 1, 0))
         return jnp.concatenate([top, bottom, end], axis=0), end_top[7:8]
 
-    def gather(t, whole):
-        first = BLOCKS * t
+    def gather(first, blocks):
         values, places = [], []
-        for i in range(BLOCKS):
-            if whole or i != mine % BLOCKS:
+        for i in range(blocks):
+            if not isinstance(first, int) or first + i != mine:
                 block_copy(first + i, (lon, lat)).wait_recv()
-        for i in range(0, BLOCKS, 2):
+        for i in range(0, blocks, 2):
             value, place = paired(first + i)
             high, rest = split(value)
             values.append(jnp.concatenate([high, rest], axis=0))
@@ -299,7 +309,7 @@
         place = jnp.concatenate(places, axis=1).astype(jnp.int32)
         across = lax.div(place, 256)
         within = lax.rem(place, 256)
-        hot = iota((256, BLOCKS * 64), 0) == within
+        hot = iota((256, blocks * 64), 0) == within
         hot = jnp.where(hot, 1.0, 0.0).astype(jnp.bfloat16)
         for q in range(0, CLON // 2, 2):
             masks = [
@@ -318,40 +328,22 @@
                 state_0[2 * (q + h) + 2] += part[:, LANES:]
 
     def gather_step(t, carry):
-        gather(t, True)
+        gather(BLOCKS * t, BLOCKS)
         return carry
 
-    ahead = FIRST
-    for t in range(0, DEVICES // BLOCKS, GROUP):
-        whole = t + GROUP < DEVICES // BLOCKS
-        lax.fori_loop(t, t + GROUP - (0 if whole else 1), gather_step, 0)
-        for m in range(ahead, min(ahead + GROUP * BLOCKS // 2, CHIPS)):
-            send_to(m)
-        ahead += GROUP * BLOCKS // 2
-    gather(DEVICES // BLOCKS - 1, False)
-
-    def pack_first(g, fields):
-        ends, near = fields
-        for k in range(UNROLL):
-            i = g * UNROLL + k
-            value = state_0[i + 1]
-            ends, near = pack_ends(i, value, ends), pack_near(i, value, near)
-        return ends, near
-
-    first = lax.fori_loop(0, CLON // UNROLL, pack_first, (nothing, nothing))
-    edge[0], near = first
-    flux[...] = jnp.zeros((CLON, LANES), jnp.float32)
-    flux_ends = few
+    lax.fori_loop(0, DEVICES // BLOCKS - 1, gather_step, 0)
+    for first in range(DEVICES - BLOCKS, DEVICES, LAST):
+        gather(first, LAST)
 
     east, west = lax.rem(lon + 1, 32), lax.rem(lon + 31, 32)
     north, south = lax.rem(lat + 1, 4), lax.rem(lat + 3, 4)
 
-    def edge_copies(s):
+    def edge_copies(s, which=range(4)):
         parts = (
+            (states[s].at[1], states[s].at[CLON + 1], (west, lat)),
+            (states[s].at[CLON], states[s].at[0], (east, lat)),
             (edge.at[s], from_south.at[s], (lon, north)),
             (edge.at[s], from_north.at[s], (lon, south)),
-            (states[s].at[1], states[s].at[CLON + 1], (west, lat)),
-            (states[s].at[CLON], states[s].at[0], (east, lat)),
         )
         return [
             pltpu.make_async_remote_copy(
@@ -362,26 +354,47 @@
                 device_id=to(*there),
             )
             for i, (source, target, there) in enumerate(parts)
+            if i in which
         ]
 
-    even = lax.rem(iota((1, LANES), 1), 2) == 0
+    for copy in edge_copies(0, range(2)):
+        copy.start()
+
+    def pack_first(g, fields):
+        ends, near = fields
+        for k in range(UNROLL):
+            i = g * UNROLL + k
+            value = state_0[i + 1]
+            ends, near = pack_ends(i, value, ends), pack_near(i, value, near)
+        return ends, near
+
+    first = lax.fori_loop(0, CLON // UNROLL, pack_first, (nothing, nothing))
+    edge[0], near = first
+    flux[...] = jnp.zeros((CLON, LANES), jnp.float32)
+    flux_ends = few
+
+    lane_row = iota((1, LANES), 1)
+    even = lax.rem(lane_row, 2) == 0
 
     for s in range(STEPS):
         now, later = states[s], states[s + 1]
-        for copy in edge_copies(s):
+        for copy in edge_copies(s, range(0 if s else 2, 4)):
             copy.start()
 
-        def row(i, ends):
-            x = now[i + 1] if ends is None else put_ends(i, ends, now[i + 1])
+        def row(i, whole):
+            x = now[i + 1]
             after, before = pltpu.roll(x, LANES - 1, 1), pltpu.roll(x, 1, 1)
+            if not whole:
+                ends = pltpu.roll(spread[...], LANES - 2 - 2 * i, 1)
+                after = jnp.where(lane_row == LANES - 2, ends, after)
+                before = jnp.where(lane_row == 1, ends, before)
             moved = transport(
                 x, now[i + 2], now[i], after, before, wind[0, i], wind[1, i]
             )
             return moved, cloud_top[pl.ds(i, 1), :], strength[pl.ds(i, 1), :]
 
         def advance_pair(i, field):
-            ends = edge[s] if s else None
-            values = convect([row(i, ends), row(i + 1, ends)], mixer[...])
+            values = convect([row(i, s == 0), row(i + 1, s == 0)], mixer[...])
             for h, value in enumerate(values):
                 later[i + h + 1] = value
                 flux[pl.ds(i + h, 1), :] += value[0:1]
@@ -417,8 +430,9 @@
             strip_wind[1],
         )
         strip = (moved, strip_top[0:1, :], strip_strength[0:1, :])
-        ends, one, two = convect([strip, row(0, None), row(CLON - 1, None)], mixer[...])
+        ends, one, two = convect([strip, row(0, True), row(CLON - 1, True)], mixer[...])
         edge[s + 1] = ends
+        spread[...] = spread_ends(ends)
         flux_ends = flux_ends + ends[0:8]
         for i, value in ((0, one), (CLON - 1, two)):
             later[i + 1] = put_ends(i, ends, value)
@@ -486,7 +500,8 @@
             pltpu.VMEM((2, LEV, LANES), f32),
             pltpu.VMEM((8, LANES), f32),
             pltpu.VMEM((8, LANES), jnp.int32),
-            pltpu.VMEM((LEV, DEPTH), jnp.bfloat16),
+            pltpu.VMEM((LEV, 3 * DEPTH), jnp.bfloat16),
+            pltpu.VMEM((LEV, LANES), f32),
             pltpu.SemaphoreType.DMA((CHIPS,)),
             pltpu.SemaphoreType.DMA,
             pltpu.SemaphoreType.DMA((DEVICES,)),

time: 76.3 us -> 72.8 us (0.954)
  Pallas kernels: 73.4 us -> 69.7 us
    pallas_call x1, Pallas kernels: 73.4 us -> 69.7 us  [on_device(): pl.pallas_call(kernel, out_shape=(pltpu.VMEM((CLON, LEV, LANES), f32), pl...]
where the time goes in v3:
time: 72.8 us; the launch traced here: 72.4 us
  Pallas kernels  69.7 us (96%)
  local copies, waits for them, and re-layouts  2.13 us (3%)
    pallas_call x1, Pallas kernels, on_device(): pl.pallas_call(kernel, out_shape=(pltpu.VMEM((CLON, LEV, LANES), f32), pl...  69.7 us
    unnamed x2, local copies, waits for them, and re-layouts  2.13 us

profile of v3, /device:TPU:1, one launch (start us, length us, event | category | flops | bytes accessed | tf_op | source)
XLA Modules:
  0.0 72.4 jit_solution(6334510758844123874)
XLA Ops:
  0.6 69.7 %shard_map.95 = (f32[48,72,128]{2,1,0:T(8,128)S(1)}, f32[48,128]{1,0:T(8,128)S(1)}) custom-call(f32[72,8192]{1,0:T(8,128)} %kernels.1, f32[64,128]{1,0:T(8,128)} %bitcast.4, s32[64,128]{1,0:T(8,128)} %bitcast.5, s32[1,128]{1,0:T(1,128)} %counts_in.1, f32[2,72,48,128]{3,2,1,0:T(8,128)} %courant.1, f32[48,128]{1,0:T(8,128)} %strength_in.1, ...), custom_call_target="tpu_custom_call" | custom-call | tf_op jit(solution)/shard_map/pallas_call | solution.py:476
  70.3 1.5 %copy.10 = f32[72,48,128]{2,1,0:T(8,128)} copy(f32[72,48,128]{2,0,1:T(8,128)S(1)} %bitcast.3) | data formatting | bytes 3538944
  71.8 0.6 copy.12

commit v4 on v3

--- a/solution.py
+++ b/solution.py
@@ -120,7 +120,9 @@
     cloud_top_in,
     redistribution_in,
     out,
+    out_ends,
     flux,
+    flux_ends,
     residuals,
     columns,
     counts,
@@ -136,7 +138,6 @@
     state_1,
     state_2,
     state_3,
-    state_4,
     edge,
     from_south,
     from_north,
@@ -152,7 +153,7 @@
     edge_send,
     edge_recv,
 ):
-    states = (state_0, state_1, state_2, state_3, state_4)
+    states = (state_0, state_1, state_2, state_3)
     lon, lat = lax.axis_index("lon"), lax.axis_index("lat")
     core = lat % 2
     at_offset = placer()
@@ -370,35 +371,47 @@
 
     first = lax.fori_loop(0, CLON // UNROLL, pack_first, (nothing, nothing))
     edge[0], near = first
+    for copy in edge_copies(0, range(2, 4)):
+        copy.start()
     flux[...] = jnp.zeros((CLON, LANES), jnp.float32)
-    flux_ends = few
+    flux_ends[...] = few
 
     lane_row = iota((1, LANES), 1)
     even = lax.rem(lane_row, 2) == 0
 
     for s in range(STEPS):
-        now, later = states[s], states[s + 1]
-        for copy in edge_copies(s, range(0 if s else 2, 4)):
-            copy.start()
-
-        def row(i, whole):
-            x = now[i + 1]
+        now = states[s]
+        last = s + 1 == STEPS
+        later = out if last else states[s + 1]
+        shift = 0 if last else 1
+
+        def row(i, halos=None):
+            x, west, east = now[i + 1], now[i], now[i + 2]
             after, before = pltpu.roll(x, LANES - 1, 1), pltpu.roll(x, 1, 1)
-            if not whole:
+            if halos:
+                above, below = halos
+                if i:
+                    west = put_ends(i - 1, edge[s], west)
+                else:
+                    east = put_ends(i + 1, edge[s], east)
+                above = pltpu.roll(above, LANES - 2 - 2 * i, 1)
+                below = pltpu.roll(below, (LANES - 2 * i) % LANES, 1)
+                after = jnp.where(lane_row == LANES - 1, above, after)
+                before = jnp.where(lane_row == 0, below, before)
+            elif s:
                 ends = pltpu.roll(spread[...], LANES - 2 - 2 * i, 1)
                 after = jnp.where(lane_row == LANES - 2, ends, after)
                 before = jnp.where(lane_row == 1, ends, before)
-            moved = transport(
-                x, now[i + 2], now[i], after, before, wind[0, i], wind[1, i]
-            )
+            moved = transport(x, east, west, after, before, wind[0, i], wind[1, i])
             return moved, cloud_top[pl.ds(i, 1), :], strength[pl.ds(i, 1), :]
 
         def advance_pair(i, field):
-            values = convect([row(i, s == 0), row(i + 1, s == 0)], mixer[...])
+            values = convect([row(i), row(i + 1)], mixer[...])
             for h, value in enumerate(values):
-                later[i + h + 1] = value
+                later[i + h + shift] = value
                 flux[pl.ds(i + h, 1), :] += value[0:1]
-                field = pack_near(i + h, value, field)
+                if not last:
+                    field = pack_near(i + h, value, field)
             return field
 
         def advance(g, field):
@@ -411,44 +424,44 @@
         for i in range(1 + 2 * groups * PAIRS, CLON - 1, 2):
             next_near = advance_pair(i, next_near)
 
+        x = edge[s]
+        near = jnp.where(even, near, pltpu.roll(near, LANES - 2, 1))
+        east_of, west_of = pltpu.roll(x, LANES - 2, 1), pltpu.roll(x, 2, 1)
         for copy in edge_copies(s):
             copy.wait_recv()
-        x = edge[s]
-        near = jnp.where(even, near, pltpu.roll(near, LANES - 2, 1))
         above = jnp.where(lat < 3, from_north[s], 0.0)
         below = jnp.where(lat > 0, from_south[s], 0.0)
-        after = jnp.where(even, pltpu.roll(above, LANES - 1, 1), near)
-        before = jnp.where(even, near, pltpu.roll(below, 1, 1))
-        around = pack_ends(CLON, now[CLON + 1], pack_ends(63, now[0], x))
+        borders = (0, CLON - 1)
+        values = convect([row(i, (above, below)) for i in borders], mixer[...])
+        for i, value in zip(borders, values):
+            later[i + shift] = value
+        if not last:
+            for copy in edge_copies(s + 1, range(2)):
+                copy.start()
         moved = transport(
             x,
-            pltpu.roll(around, LANES - 2, 1),
-            pltpu.roll(around, 2, 1),
-            after,
-            before,
+            pack_ends(CLON - 1, now[CLON + 1], east_of),
+            pack_ends(0, now[0], west_of),
+            jnp.where(even, pltpu.roll(above, LANES - 1, 1), near),
+            jnp.where(even, near, pltpu.roll(below, 1, 1)),
             strip_wind[0],
             strip_wind[1],
         )
         strip = (moved, strip_top[0:1, :], strip_strength[0:1, :])
-        ends, one, two = convect([strip, row(0, True), row(CLON - 1, True)], mixer[...])
-        edge[s + 1] = ends
-        spread[...] = spread_ends(ends)
-        flux_ends = flux_ends + ends[0:8]
-        for i, value in ((0, one), (CLON - 1, two)):
-            later[i + 1] = put_ends(i, ends, value)
+        (ends,) = convect([strip], mixer[...])
+        flux_ends[...] += ends[0:8]
+        if last:
+            out_ends[...] = ends
+        else:
+            edge[s + 1] = ends
+            for copy in edge_copies(s + 1, range(2, 4)):
+                copy.start()
+            spread[...] = spread_ends(ends)
+        for i, value in zip(borders, values):
             flux[pl.ds(i, 1), :] += value[0:1]
-            next_near = pack_near(i, value, next_near)
+            if not last:
+                next_near = pack_near(i, value, next_near)
         near = next_near
-
-    def finish(g, carry):
-        for k in range(UNROLL):
-            i = g * UNROLL + k
-            out[i] = put_ends(i, edge[STEPS], state_4[i + 1])
-            total = jnp.broadcast_to(flux[pl.ds(i, 1), :], (8, LANES))
-            flux[pl.ds(i, 1), :] = put_ends(i, flux_ends, total)[0:1]
-        return carry
-
-    lax.fori_loop(0, CLON // UNROLL, finish, 0)
 
     def sent(k, carry):
         block_copy(k, (lon, lat)).wait_send()
@@ -459,6 +472,23 @@
     for s in range(STEPS):
         for copy in edge_copies(s):
             copy.wait_send()
+
+
+def finish(field, ends, flux_in, flux_ends, out, flux, whole, whole_flux, sem, flux_sem):
+    def group(g, carry):
+        for k in range(UNROLL):
+            i = g * UNROLL + k
+            whole[i] = put_ends(i, ends[...], field[i])
+            pltpu.make_async_copy(whole.at[i], out.at[:, i, :], sem).start()
+            total = jnp.broadcast_to(flux_in[pl.ds(i, 1), :], (8, LANES))
+            whole_flux[pl.ds(i, 1), :] = put_ends(i, flux_ends[...], total)[0:1]
+        return carry
+
+    lax.fori_loop(0, CLON // UNROLL, group, 0)
+    last = pltpu.make_async_copy(whole_flux, flux, flux_sem)
+    last.start()
+    pltpu.make_async_copy(out, out, sem).wait()
+    last.wait()
 
 
 def on_device(
@@ -473,14 +503,16 @@
 ):
     in_vmem = pl.BlockSpec(memory_space=pltpu.VMEM)
     f32 = jnp.float32
-    field, flux = pl.pallas_call(
+    parts = pl.pallas_call(
         kernel,
         out_shape=(
             pltpu.VMEM((CLON, LEV, LANES), f32),
+            pltpu.VMEM((LEV, LANES), f32),
             pltpu.VMEM((CLON, LANES), f32),
+            pltpu.VMEM((8, LANES), f32),
         ),
         in_specs=[pl.BlockSpec(memory_space=pl.ANY)] * 8,
-        out_specs=(in_vmem, in_vmem),
+        out_specs=(in_vmem,) * 4,
         scratch_shapes=[
             pltpu.VMEM((CHIPS, LANES), f32),
             pltpu.VMEM((CHIPS, LANES), jnp.int32),
@@ -493,8 +525,8 @@
             pltpu.VMEM((2, CLON, LEV, LANES), f32),
             pltpu.VMEM((DEVICES, ROWS, LANES), f32),
             pltpu.VMEM((DEVICES, ROWS, LANES), f32),
-            *[pltpu.VMEM((CLON + 2, LEV, LANES), f32) for _ in range(STEPS + 1)],
-            pltpu.VMEM((STEPS + 1, LEV, LANES), f32),
+            *[pltpu.VMEM((CLON + 2, LEV, LANES), f32) for _ in range(STEPS)],
+            pltpu.VMEM((STEPS, LEV, LANES), f32),
             pltpu.VMEM((STEPS, LEV, LANES), f32),
             pltpu.VMEM((STEPS, LEV, LANES), f32),
             pltpu.VMEM((2, LEV, LANES), f32),
@@ -527,7 +559,22 @@
             )
         )
     )
-    return field.transpose(1, 0, 2), flux
+    return pl.pallas_call(
+        finish,
+        out_shape=(
+            jax.ShapeDtypeStruct((LEV, CLON, LANES), f32),
+            jax.ShapeDtypeStruct((CLON, LANES), f32),
+        ),
+        in_specs=[in_vmem] * 4,
+        out_specs=(pl.BlockSpec(memory_space=pl.ANY),) * 2,
+        scratch_shapes=[
+            pltpu.VMEM((CLON, LEV, LANES), f32),
+            pltpu.VMEM((CLON, LANES), f32),
+            pltpu.SemaphoreType.DMA,
+            pltpu.SemaphoreType.DMA,
+        ],
+        compiler_params=pltpu.CompilerParams(vmem_limit_bytes=16 * 2**20),
+    )(*parts)
 
 
 def solution(mesh):

time: 72.8 us -> 71.6 us (0.984)
  local copies, waits for them, and re-layouts: 2.13 us -> 0 us
    unnamed x2 -> x0, local copies, waits for them, and re-layouts: 2.13 us -> none
    pallas_call x0 -> x1, Pallas kernels: none -> 1.7 us  [on_device(): pl.pallas_call(finish, out_shape=(jax.ShapeDtypeStruct((LEV, CLON, LANES)...]
    pallas_call x1, Pallas kernels: 69.7 us -> 68.7 us  [on_device(): pl.pallas_call(kernel, out_shape=(pltpu.VMEM((CLON, LEV, LANES), f32), pl...]
where the time goes in v4:
time: 71.6 us; the launch traced here: 71.2 us
  Pallas kernels  70.4 us (98%)
  between operations  0.8 us (1%)
    pallas_call x1, Pallas kernels, on_device(): pl.pallas_call(kernel, out_shape=(pltpu.VMEM((CLON, LEV, LANES), f32), pl...  68.7 us
    pallas_call x1, Pallas kernels, on_device(): pl.pallas_call(finish, out_shape=(jax.ShapeDtypeStruct((LEV, CLON, LANES)...  1.7 us

profile of v4, /device:TPU:1, one launch (start us, length us, event | category | flops | bytes accessed | tf_op | source)
XLA Modules:
  0.0 71.2 jit_solution(13016079871642924485)
XLA Ops:
  0.6 68.7 %shard_map.95 = (f32[48,72,128]{2,1,0:T(8,128)S(1)}, f32[72,128]{1,0:T(8,128)S(1)}, f32[48,128]{1,0:T(8,128)S(1)}, f32[8,128]{1,0:T(8,128)S(1)}) custom-call(f32[72,8192]{1,0:T(8,128)} %kernels.1, f32[64,128]{1,0:T(8,128)} %bitcast.2, s32[64,128]{1,0:T(8,128)} %bitcast.3, s32[1,128]{1,0:T(1,128)} %counts_in.1, f32[2,72,48,128]{3,2,1,0:T(8,128)} %courant.1, ...), custom_call_target="tpu_custom_call" | custom-call | tf_op jit(solution)/shard_map/pallas_call | solution.py:506
  69.4 1.7 %shard_map.96 = (f32[72,48,128]{2,1,0:T(8,128)}, f32[48,128]{1,0:T(8,128)}) custom-call(f32[48,72,128]{2,1,0:T(8,128)S(1)} %get-tuple-element.6.field, f32[72,128]{1,0:T(8,128)S(1)} %get-tuple-element.7.ends, f32[48,128]{1,0:T(8,128)S(1)} %get-tuple-element.8.flux_in, f32[8,128]{1,0:T(8,128)S(1)} %get-tuple-element.9.flux_ends), custom_call_target="tpu_custom_call" | custom-call | tf_op jit(solution)/shard_map/pallas_call | solution.py:562

commit v5 on v4

--- a/solution.py
+++ b/solution.py
@@ -16,15 +16,17 @@
 DEVICES = 128
 ROWS = 37
 BLOCKS = 8
-UNROLL = 6
+UNROLL = 12
 PAIRS = 11
-LAST = 4
+LAST = 8
 DEPTH = 80
 
 OFFSETS = list(itertools.product(range(4), repeat=3))
 random.Random(1).shuffle(OFFSETS)
-OFFSETS.sort(key=lambda o: sum(min(v, 4 - v) for v in o))
-OFFSETS = OFFSETS[1:] + OFFSETS[:1]
+JITTER = random.Random(1)
+OFFSETS.sort(key=lambda o: sum(min(v, 4 - v) for v in o) + JITTER.random() * 1.5)
+OFFSETS.remove((0, 0, 0))
+OFFSETS.append((0, 0, 0))
 
 
 def coords():
@@ -296,46 +298,6 @@
         end = jnp.where(sub < 4, pltpu.roll(end_top, 5, 0), pltpu.roll(end_bottom, 1, 0))
         return jnp.concatenate([top, bottom, end], axis=0), end_top[7:8]
 
-    def gather(first, blocks):
-        values, places = [], []
-        for i in range(blocks):
-            if not isinstance(first, int) or first + i != mine:
-                block_copy(first + i, (lon, lat)).wait_recv()
-        for i in range(0, blocks, 2):
-            value, place = paired(first + i)
-            high, rest = split(value)
-            values.append(jnp.concatenate([high, rest], axis=0))
-            places.append(place)
-        both = jnp.concatenate(values, axis=1).astype(jnp.bfloat16)
-        place = jnp.concatenate(places, axis=1).astype(jnp.int32)
-        across = lax.div(place, 256)
-        within = lax.rem(place, 256)
-        hot = iota((256, blocks * 64), 0) == within
-        hot = jnp.where(hot, 1.0, 0.0).astype(jnp.bfloat16)
-        for q in range(0, CLON // 2, 2):
-            masks = [
-                jnp.where(across == q + h, 1.0, 0.0).astype(jnp.bfloat16) for h in range(2)
-            ]
-            put = lax.dot_general(
-                jnp.concatenate([both * mask for mask in masks], axis=0),
-                hot,
-                (((1,), (1,)), ((), ())),
-                preferred_element_type=jnp.float32,
-            )
-            for h in range(2):
-                part = put[2 * h * LEV : (2 * h + 1) * LEV]
-                part = part + put[(2 * h + 1) * LEV : (2 * h + 2) * LEV]
-                state_0[2 * (q + h) + 1] += part[:, :LANES]
-                state_0[2 * (q + h) + 2] += part[:, LANES:]
-
-    def gather_step(t, carry):
-        gather(BLOCKS * t, BLOCKS)
-        return carry
-
-    lax.fori_loop(0, DEVICES // BLOCKS - 1, gather_step, 0)
-    for first in range(DEVICES - BLOCKS, DEVICES, LAST):
-        gather(first, LAST)
-
     east, west = lax.rem(lon + 1, 32), lax.rem(lon + 31, 32)
     north, south = lax.rem(lat + 1, 4), lax.rem(lat + 3, 4)
 
@@ -358,8 +320,50 @@
             if i in which
         ]
 
-    for copy in edge_copies(0, range(2)):
-        copy.start()
+    order = [0, CLON // 2 - 1, *range(1, CLON // 2 - 1)]
+
+    def gather(first, blocks):
+        values, places = [], []
+        for i in range(blocks):
+            if not isinstance(first, int) or first + i != mine:
+                block_copy(first + i, (lon, lat)).wait_recv()
+        for i in range(0, blocks, 2):
+            value, place = paired(first + i)
+            high, rest = split(value)
+            values.append(jnp.concatenate([high, rest], axis=0))
+            places.append(place)
+        both = jnp.concatenate(values, axis=1).astype(jnp.bfloat16)
+        place = jnp.concatenate(places, axis=1).astype(jnp.int32)
+        across = lax.div(place, 256)
+        within = lax.rem(place, 256)
+        hot = iota((256, blocks * 64), 0) == within
+        hot = jnp.where(hot, 1.0, 0.0).astype(jnp.bfloat16)
+        for pairs in zip(order[::2], order[1::2]):
+            masks = [
+                jnp.where(across == q, 1.0, 0.0).astype(jnp.bfloat16) for q in pairs
+            ]
+            put = lax.dot_general(
+                jnp.concatenate([both * mask for mask in masks], axis=0),
+                hot,
+                (((1,), (1,)), ((), ())),
+                preferred_element_type=jnp.float32,
+            )
+            for h, q in enumerate(pairs):
+                part = put[2 * h * LEV : (2 * h + 1) * LEV]
+                part = part + put[(2 * h + 1) * LEV : (2 * h + 2) * LEV]
+                state_0[2 * q + 1] += part[:, :LANES]
+                state_0[2 * q + 2] += part[:, LANES:]
+            if pairs[0] == 0 and isinstance(first, int) and first + blocks == DEVICES:
+                for copy in edge_copies(0, range(2)):
+                    copy.start()
+
+    def gather_step(t, carry):
+        gather(BLOCKS * t, BLOCKS)
+        return carry
+
+    lax.fori_loop(0, DEVICES // BLOCKS - 1, gather_step, 0)
+    for first in range(DEVICES - BLOCKS, DEVICES, LAST):
+        gather(first, LAST)
 
     def pack_first(g, fields):
         ends, near = fields

time: 71.6 us -> 70.2 us (0.980)
  Pallas kernels: 70.4 us -> 69 us
    pallas_call x1, Pallas kernels: 68.7 us -> 67.6 us  [on_device(): pl.pallas_call(kernel, out_shape=(pltpu.VMEM((CLON, LEV, LANES), f32), pl...]
where the time goes in v5:
time: 70.2 us; the launch traced here: 69.8 us
  Pallas kernels  69 us (98%)
  between operations  0.8 us (1%)
    pallas_call x1, Pallas kernels, on_device(): pl.pallas_call(kernel, out_shape=(pltpu.VMEM((CLON, LEV, LANES), f32), pl...  67.6 us
    pallas_call x1, Pallas kernels, on_device(): pl.pallas_call(finish, out_shape=(jax.ShapeDtypeStruct((LEV, CLON, LANES)...  1.44 us

profile of v5, /device:TPU:1, one launch (start us, length us, event | category | flops | bytes accessed | tf_op | source)
XLA Modules:
  0.0 69.8 jit_solution(16880622758007881266)
XLA Ops:
  0.6 67.6 %shard_map.95 = (f32[48,72,128]{2,1,0:T(8,128)S(1)}, f32[72,128]{1,0:T(8,128)S(1)}, f32[48,128]{1,0:T(8,128)S(1)}, f32[8,128]{1,0:T(8,128)S(1)}) custom-call(f32[72,8192]{1,0:T(8,128)} %kernels.1, f32[64,128]{1,0:T(8,128)} %bitcast.2, s32[64,128]{1,0:T(8,128)} %bitcast.3, s32[1,128]{1,0:T(1,128)} %counts_in.1, f32[2,72,48,128]{3,2,1,0:T(8,128)} %courant.1, ...), custom_call_target="tpu_custom_call" | custom-call | tf_op jit(solution)/shard_map/pallas_call | solution.py:510
  68.2 1.4 %shard_map.96 = (f32[72,48,128]{2,1,0:T(8,128)}, f32[48,128]{1,0:T(8,128)}) custom-call(f32[48,72,128]{2,1,0:T(8,128)S(1)} %get-tuple-element.6.field, f32[72,128]{1,0:T(8,128)S(1)} %get-tuple-element.7.ends, f32[48,128]{1,0:T(8,128)S(1)} %get-tuple-element.8.flux_in, f32[8,128]{1,0:T(8,128)S(1)} %get-tuple-element.9.flux_ends), custom_call_target="tpu_custom_call" | custom-call | tf_op jit(solution)/shard_map/pallas_call | solution.py:566

commit v6 on v5

--- a/solution.py
+++ b/solution.py
@@ -383,6 +383,10 @@
     lane_row = iota((1, LANES), 1)
     even = lax.rem(lane_row, 2) == 0
 
+    def sent(k, carry):
+        block_copy(k, (lon, lat)).wait_send()
+        return carry
+
     for s in range(STEPS):
         now = states[s]
         last = s + 1 == STEPS
@@ -427,6 +431,14 @@
         next_near = lax.fori_loop(0, groups, advance, nothing)
         for i in range(1 + 2 * groups * PAIRS, CLON - 1, 2):
             next_near = advance_pair(i, next_near)
+
+        share = DEVICES // STEPS
+        lax.fori_loop(share * s, min(share * (s + 1), mine), sent, 0)
+        if last:
+            block_copy(DEVICES - 1, (lon, lat)).wait_send()
+        if s:
+            for copy in edge_copies(s - 1):
+                copy.wait_send()
 
         x = edge[s]
         near = jnp.where(even, near, pltpu.roll(near, LANES - 2, 1))
@@ -467,15 +479,8 @@
                 next_near = pack_near(i, value, next_near)
         near = next_near
 
-    def sent(k, carry):
-        block_copy(k, (lon, lat)).wait_send()
-        return carry
-
-    lax.fori_loop(0, mine, sent, 0)
-    block_copy(DEVICES - 1, (lon, lat)).wait_send()
-    for s in range(STEPS):
-        for copy in edge_copies(s):
-            copy.wait_send()
+    for copy in edge_copies(STEPS - 1):
+        copy.wait_send()
 
 
 def finish(field, ends, flux_in, flux_ends, out, flux, whole, whole_flux, sem, flux_sem):

time: 70.2 us -> 69.9 us (level)
  no operation moved by 1% of the time
where the time goes in v6:
time: 69.9 us; the launch traced here: 69.6 us
  Pallas kernels  68.8 us (98%)
  between operations  0.8 us (1%)
    pallas_call x1, Pallas kernels, on_device(): pl.pallas_call(kernel, out_shape=(pltpu.VMEM((CLON, LEV, LANES), f32), pl...  67.3 us
    pallas_call x1, Pallas kernels, on_device(): pl.pallas_call(finish, out_shape=(jax.ShapeDtypeStruct((LEV, CLON, LANES)...  1.44 us

profile of v6, /device:TPU:1, one launch (start us, length us, event | category | flops | bytes accessed | tf_op | source)
XLA Modules:
  0.0 69.6 jit_solution(4229589404746853675)
XLA Ops:
  0.6 67.3 %shard_map.95 = (f32[48,72,128]{2,1,0:T(8,128)S(1)}, f32[72,128]{1,0:T(8,128)S(1)}, f32[48,128]{1,0:T(8,128)S(1)}, f32[8,128]{1,0:T(8,128)S(1)}) custom-call(f32[72,8192]{1,0:T(8,128)} %kernels.1, f32[64,128]{1,0:T(8,128)} %bitcast.2, s32[64,128]{1,0:T(8,128)} %bitcast.3, s32[1,128]{1,0:T(1,128)} %counts_in.1, f32[2,72,48,128]{3,2,1,0:T(8,128)} %courant.1, ...), custom_call_target="tpu_custom_call" | custom-call | tf_op jit(solution)/shard_map/pallas_call | solution.py:515
  68.0 1.4 %shard_map.96 = (f32[72,48,128]{2,1,0:T(8,128)}, f32[48,128]{1,0:T(8,128)}) custom-call(f32[48,72,128]{2,1,0:T(8,128)S(1)} %get-tuple-element.6.field, f32[72,128]{1,0:T(8,128)S(1)} %get-tuple-element.7.ends, f32[48,128]{1,0:T(8,128)S(1)} %get-tuple-element.8.flux_in, f32[8,128]{1,0:T(8,128)S(1)} %get-tuple-element.9.flux_ends), custom_call_target="tpu_custom_call" | custom-call | tf_op jit(solution)/shard_map/pallas_call | solution.py:571
